TPU v7x, 512 devices: a whole 4x8x8 slice. The times are simulated.
512 devices in a mesh: blk: 16 (over z_lo, x), head: 32 (over y, z_hi, core).
Axes of the slice: x: 4, y: 8, z: 8 (z_hi: 2, z_lo: 4; z = z_hi * 4 + z_lo), core: 2. Of those that a mesh axis runs over, the one named last changes fastest.
Arguments:
- queries: bfloat16 [32768, 12288], P(('blk', 'head')), may hold values from -64 to 64, as said below
- exponents: int32 [32768, 64], P(('blk', 'head')), may hold values from -2 to 2
- latent: bfloat16 [32768, 576], P(('blk', 'head')), may hold values from -6 to 6, as said below
- segments: int32 [32768], P(('blk', 'head')), may hold values from 0 to 47, never falling along the last dimension, each value on 1 to 1024 neighbouring positions
- key_weight: bfloat16 [512, 8192], P(None, 'head'), may hold values from -0.25 to 0.25
- value_weight: bfloat16 [512, 8192], P(None, 'head'), may hold values from -0.25 to 0.25
Outputs:
- attended: bfloat16 [32768, 8192], P(('blk', 'head'))
Inputs may be any that keep to these rules, and one draw needn't show every extreme that they name: queries stay within the range. `latent`: latents stay within the range. `segments`: document numbers never fall along the sequence, and a document holds at most 1024 tokens.
All inputs are finite; a program needn't handle non-finite values.
Results may differ from a plain program's by a relative error of at most 0.0069.
Values may be sent and summed in bfloat16 or wider, within the bound.
A program may use at most 64 MiB of HBM per device.

v0:
```python
import math

import jax
import jax.numpy as jnp
from jax import lax
from jax.sharding import Mesh
from jax.sharding import PartitionSpec as P

NOPE = 128
ROPE = 64
LATENT = 512
VDIM = 128
HEAD = ("head_0", "head_1", "head_2")
BLK_HEAD = ("blk", "head_0", "head_1", "head_2")


neg_large = -1e30


def passed_along(block, axis, distance):
    devices = range(lax.axis_size(axis))
    route = [(i - distance, i) for i in devices if i - distance in devices]
    return lax.ppermute(block, axis, route)


def laid_out(blocks, dim):
    lengths = list(blocks.shape[1:])
    lengths[dim] *= blocks.shape[0]
    return jnp.moveaxis(blocks, 0, dim).reshape(lengths)


def all_blocks(value, axes, order):
    blocks = value
    for k in order:
        blocks = lax.all_gather(blocks, axes[k])
    done = order[::-1]
    back = [done.index(k) for k in range(len(axes))]
    blocks = blocks.transpose(*back, *range(len(axes), blocks.ndim))
    return blocks.reshape(-1, *value.shape)


def whole_of(value, axes, order, dim):
    return laid_out(all_blocks(value, axes, order), dim)


def power_two(exponent):
    result = jnp.zeros(exponent.shape, jnp.float32)
    for level in range(-4, 5):
        result = result + jnp.where(exponent == level, jnp.float32(2.0**level), jnp.float32(0.0))
    return result


def body(queries, exponents, latent, segments, key_weight, value_weight):
    row_count = queries.shape[0]
    head_total = exponents.shape[1]
    width = queries.shape[1] // head_total
    shaped = queries.reshape(row_count, head_total, width)
    moved, powers = (
        lax.all_to_all(shaped, HEAD, split_axis=1, concat_axis=0, tiled=True),
        lax.all_to_all(exponents, HEAD, split_axis=1, concat_axis=0, tiled=True),
    )
    group = moved.shape[0]
    local_heads = moved.shape[1]
    scaled = (moved.astype(jnp.float32) * power_two(powers)[:, :, None]).astype(jnp.bfloat16)
    softmax_scale = 1.0 / math.sqrt(NOPE + ROPE)
    block = min(512, group)
    longest = group // 2
    lead = (longest - 1 + block - 1) // block * block
    cycle_place = lax.axis_index("blk")
    earlier, earlier_seg = passed_along((latent, segments), "blk", 1)
    own, own_seg, before, before_seg = (
        whole_of(latent, HEAD, (1, 0, 2), 0),
        whole_of(segments, HEAD, (1, 0, 2), 0),
        whole_of(earlier, HEAD, (1, 0, 2), 0),
        whole_of(earlier_seg, HEAD, (1, 0, 2), 0),
    )
    before_rows = before[group - lead :]
    before_ids = before_seg[group - lead :]
    window = jnp.concatenate([before_rows, own], axis=0)
    window_seg = jnp.concatenate([before_ids, own_seg], axis=0)
    window_rows = lead + group
    window_pos = cycle_place * group - lead + jnp.arange(window_rows, dtype=jnp.int32)
    query_pos = cycle_place * group + jnp.arange(group, dtype=jnp.int32)
    compressed = window[:, :LATENT]
    rope_keys = window[:, LATENT:]
    keys = jnp.dot(compressed, key_weight, preferred_element_type=jnp.float32).astype(jnp.bfloat16)
    keys = keys.reshape(window_rows, local_heads, NOPE)
    values = jnp.dot(compressed, value_weight, preferred_element_type=jnp.float32).astype(
        jnp.bfloat16
    )
    values = values.reshape(window_rows, local_heads, VDIM)

    def one_block(index):
        start = index * block
        query_nope = lax.dynamic_slice_in_dim(scaled, start, block, 0)[:, :, :NOPE]
        query_rope = lax.dynamic_slice_in_dim(scaled, start, block, 0)[:, :, NOPE:]
        query_seg = lax.dynamic_slice_in_dim(own_seg, start, block, 0)
        query_here = lax.dynamic_slice_in_dim(query_pos, start, block, 0)
        key_rows = lax.dynamic_slice_in_dim(keys, start, lead + block, 0)
        rope_rows = lax.dynamic_slice_in_dim(rope_keys, start, lead + block, 0)
        value_rows = lax.dynamic_slice_in_dim(values, start, lead + block, 0)
        key_seg = lax.dynamic_slice_in_dim(window_seg, start, lead + block, 0)
        key_here = lax.dynamic_slice_in_dim(window_pos, start, lead + block, 0)
        allowed = (
            (query_seg[:, None] == key_seg[None, :])
            & (key_here[None, :] <= query_here[:, None])
            & (key_here[None, :] >= 0)
        )
        scores = jnp.einsum(
            "ghd,khd->hgk", query_nope, key_rows, preferred_element_type=jnp.float32
        )
        scores = scores + jnp.einsum(
            "ghd,kd->hgk", query_rope, rope_rows, preferred_element_type=jnp.float32
        )
        scores = jnp.where(allowed[None], scores * softmax_scale, neg_large)
        largest = jnp.max(scores, axis=2, keepdims=True)
        weights = jnp.where(allowed[None], jnp.exp(scores - largest), 0.0)
        sums = jnp.sum(weights, axis=2)
        weighted = jnp.einsum(
            "hgk,khd->ghd",
            weights.astype(jnp.bfloat16),
            value_rows,
            preferred_element_type=jnp.float32,
        )
        return (weighted / sums.T[:, :, None]).astype(jnp.bfloat16)

    blocks = lax.map(one_block, jnp.arange(group // block, dtype=jnp.int32))
    result = blocks.reshape(group, local_heads, VDIM)
    returned = lax.all_to_all(result, HEAD, split_axis=0, concat_axis=1, tiled=True)
    return returned.reshape(row_count, head_total * VDIM)


def solution(mesh):
    split = Mesh(
        mesh.devices.reshape(mesh.shape["blk"], 8, 2, 2), ("blk", "head_0", "head_1", "head_2")
    )
    placed = (
        P(BLK_HEAD, None),
        P(BLK_HEAD, None),
        P(BLK_HEAD, None),
        P(BLK_HEAD),
        P(None, HEAD),
        P(None, HEAD),
    )
    return jax.shard_map(
        body, mesh=split, in_specs=placed, out_specs=P(BLK_HEAD, None), check_vma=False
    )
```

profile of v0, /device:TPU:1, one launch (start us, length us, event | category | flops | bytes accessed | tf_op | source)
XLA Modules:
  0.0 325.7 jit_solution(10049185255265756133)
XLA Ops:
  6.5 14.1 %all-gather.3 = bf16[128,576]{1,0:T(8,128)(2,1)} all-gather(bf16[64,576]{1,0:T(8,128)(2,1)} %param.10), channel_id=5, replica_groups=mesh['blk'=16,'head_0'=8,'head_1'=2,'head_2'=2] {'head_1'}, dimensions={0}, use_global_device_ids=true | all-gather | bytes 221184 | tf_op jit(solution)/shard_map/all_gather | solution.py:35
  20.7 3.4 %collective-permute-start = (bf16[64,576]{1,0:T(8,128)(2,1)}, bf16[64,576]{1,0:T(8,128)(2,1)S(1)}, u32[]{:S(2)}, u32[]{:S(2)}) collective-permute-start(bf16[64,576]{1,0:T(8,128)(2,1)} %param.10), channel_id=1, source_target_pairs={{0,32},{32,64},{64,96},{96,128},{128,160},{160,192},{192,224},{224... | collective-permute-start | bytes 221192 | tf_op jit(solution)/shard_map/ppermute | solution.py:23
  25.8 8.0 %all-gather = bf16[128,576]{1,0:T(8,128)(2,1)} all-gather(bf16[64,576]{1,0:T(8,128)(2,1)S(1)} %collective-permute-done), channel_id=2, replica_groups=mesh['blk'=16,'head_0'=8,'head_1'=2,'head_2'=2] {'head_1'}, dimensions={0}, use_global_device_ids=true | all-gather | bytes 221184 | tf_op jit(solution)/shard_map/all_gather | solution.py:35
  33.9 26.8 %all-gather.23.cloned.1.call-done = bf16[16,64,576]{2,1,0:T(8,128)(2,1)} async-done(((bf16[2,64,576]{2,1,0:T(8,128)(2,1)}), bf16[16,64,576]{2,1,0:T(8,128)(2,1)}) %all-gather.23.cloned.1.call-update) | async-done | bytes 1179664 | tf_op jit(solution)/shard_map/all_gather | solution.py:35
  62.3 14.8 %all-to-all-start.1 = ((s32[32,1,128]{2,1,0:T(1,128)}), s32[32,1,128]{2,1,0:T(1,128)S(1)}, u32[]{:S(2)}, u32[]{:S(2)}) async-start(s32[32,1,128]{2,1,0:T(1,128)} %reshape.246), calls=%async_computation.1 | async-start | bytes 32768 | tf_op jit(solution)/shard_map/all_to_all | solution.py:60
  77.1 3.6 %reshape.203 = bf16[64,64,192]{2,1,0:T(8,128)(2,1)S(1)} reshape(bf16[64,12288]{1,0:T(8,128)(2,1)} %param.8) | data formatting | bytes 3145728 | tf_op jit(solution)/shard_map/reshape | solution.py:57
  83.2 5.6 %all-to-all-done.1 = s32[32,1,128]{2,1,0:T(1,128)S(1)} async-done(((s32[32,1,128]{2,1,0:T(1,128)}), s32[32,1,128]{2,1,0:T(1,128)S(1)}, u32[]{:S(2)}, u32[]{:S(2)}) %all-to-all-start.1) | async-done | bytes 16416 | tf_op jit(solution)/shard_map/all_to_all | solution.py:60
  88.8 6.7 %all-to-all-start = ((bf16[64,64,192]{2,0,1:T(8,128)(2,1)}), bf16[64,64,192]{2,0,1:T(8,128)(2,1)S(1)}, u32[]{:S(2)}, u32[]{:S(2)}) async-start(bf16[64,64,192]{2,0,1:T(8,128)(2,1)} %copy.41), calls=%async_computation | async-start | bytes 4194304 | tf_op jit(solution)/shard_map/all_to_all | solution.py:59
  95.6 11.2 %all-gather.19.cloned.1.call-done = bf16[16,64,576]{2,1,0:T(8,128)(2,1)} async-done(((bf16[2,64,576]{2,1,0:T(8,128)(2,1)}), bf16[16,64,576]{2,1,0:T(8,128)(2,1)}) %all-gather.19.cloned.1.call-update) | async-done | bytes 1179664 | tf_op jit(solution)/shard_map/all_gather | solution.py:35
  106.9 3.1 collective-permute-start.1
  112.4 14.6 %all-reduce.2 = (s32[128]{0:T(128)S(1)}, s32[128]{0:T(128)S(1)}) all-reduce(s32[128]{0:T(128)S(1)} %dynamic-update-slice, s32[128]{0:T(128)S(1)} %dynamic-update-slice.1), channel_id=8, replica_groups=mesh['blk'=16,'head_0'=8,'head_1'=2,'head_2'=2] {'head_1'}, use_global_device_ids=true, to_apply=%add | all-reduce | flops 256 | bytes 2048
  127.1 29.0 %all-gather.12 = s32[8,2,64]{2,1,0:T(2,128)S(1)} all-gather(s32[1,2,64]{2,1,0:T(2,128)S(1)} %reshape.233), channel_id=9, replica_groups=mesh['blk'=16,'head_0'=8,'head_1'=2,'head_2'=2] {'head_0'}, dimensions={0}, use_global_device_ids=true | all-gather | bytes 4608 | tf_op jit(solution)/shard_map/all_gather | solution.py:35
  156.1 4.1 %all-gather.8 = s32[16,2,64]{2,1,0:T(2,128)S(1)} all-gather(s32[8,2,64]{2,1,0:T(2,128)S(1)} %all-gather.12), channel_id=10, replica_groups=mesh['blk'=16,'head_0'=8,'head_1'=2,'head_2'=2] {'head_2'}, dimensions={0}, use_global_device_ids=true | all-gather | bytes 12288 | tf_op jit(solution)/shard_map/all_gather | solution.py:35
  160.4 9.9 %all-gather.13 = s32[8,2,64]{2,1,0:T(2,128)S(1)} all-gather(s32[1,2,64]{2,1,0:T(2,128)S(1)} %reshape.235), channel_id=12, replica_groups=mesh['blk'=16,'head_0'=8,'head_1'=2,'head_2'=2] {'head_0'}, dimensions={0}, use_global_device_ids=true | all-gather | bytes 4608 | tf_op jit(solution)/shard_map/all_gather | solution.py:35
  170.3 5.2 %all-gather.11 = s32[16,2,64]{2,1,0:T(2,128)S(1)} all-gather(s32[8,2,64]{2,1,0:T(2,128)S(1)} %all-gather.13), channel_id=13, replica_groups=mesh['blk'=16,'head_0'=8,'head_1'=2,'head_2'=2] {'head_2'}, dimensions={0}, use_global_device_ids=true | all-gather | bytes 12288 | tf_op jit(solution)/shard_map/all_gather | solution.py:35
  185.0 4.0 %convolution_convert_fusion.1 = bf16[3072,256]{0,1:T(8,128)(2,1)} fusion(bf16[512,256]{1,0:T(8,128)(2,1)S(1)} %copy-done, bf16[1024,576]{1,0:T(8,128)(2,1)S(1)} %bitcast.88, bf16[2048,576]{1,0:T(8,128)(2,1)S(1)} %bitcast.84), kind=kOutput, calls=%fused_computation.30 | convolution fusion | flops 812384256 | bytes 5373952 | tf_op jit(solution)/shard_map/dot_general | solution.py:88
  189.0 4.0 %convolution_convert_fusion = bf16[3072,256]{0,1:T(8,128)(2,1)} fusion(bf16[512,256]{1,0:T(8,128)(2,1)S(1)} %copy-done.1, bf16[1024,576]{1,0:T(8,128)(2,1)S(1)} %bitcast.89, bf16[2048,576]{1,0:T(8,128)(2,1)S(1)} %bitcast.85), kind=kOutput, calls=%fused_computation.29 | convolution fusion | flops 812384256 | bytes 5373952 | tf_op jit(solution)/shard_map/dot_general | solution.py:86
  194.4 77.1 %while.10 = (s32[]{:T(128)}, bf16[4,512,2,128]{3,1,0,2:T(8,128)(2,1)}, s32[4]{0:T(128)S(1)}, bf16[3072,2,128]{0,2,1:T(8,128)(2,1)}, s32[2048]{0:T(1024)S(1)}, /*...) while((s32[]{:T(128)}, ...), condition=%wide.region_3.4_spmd, body=%wide.region_0.3_spmd.sunk | while | flops 1021053952 | bytes 24899364 | solution.py:127
  195.7 4.6 %fusion.63 = f32[1536,512,2]{0,1,2:T(8,128)} fusion(bf16[2048,2,192]{2,0,1:T(8,128)(2,1)} %get-tuple-element.256, s32[]{:T(128)S(6)} %select_n.248, s32[]{:T(128)S(6)} %add.230, bf16[3072,64]{0,1:T(8,128)(2,1)S(1)} %get-tuple-element.258, s32[]{:T(128)S(6)} %select_n.247), kind=kOutput, calls=%fused_computation.14.clone.1 | convolution fusion | flops 201326592 | bytes 6750220 | tf_op jit(solution)/shard_map/while/body/eval_jaxpr/ghd,kd->hgk/dot_general | solution.py:112
  201.4 8.1 %fusion.64 = (f32[2,512]{1,0:T(2,128)S(1)}, bf16[2,512,1536]{2,1,0:T(8,128)(2,1)}) fusion(pred[512,1536]{1,0:T(8,128)(4,1)S(1)} %and_and_fusion.2, f32[1536,512,2]{0,1,2:T(8,128)} %fusion.63, bf16[3072,2,128]{0,2,1:T(8,128)(2,1)} %get-tuple-element.257, s32[]{:T(128)S(6)} %select_n.247, bf16[2048,2,192]{2,0,1:T(8,128)(2,1)} %get-tuple-element.256, ...), kind=kOutput, calls=%fused_computation.56.clone.1 | convolution fusion | flops 413664768 | bytes 12062728 | tf_op jit(solution)/shard_map/while/body/eval_jaxpr/sub | solution.py:117
  209.5 3.3 %fusion.65 = bf16[1,512,2,128]{1,3,2,0:T(8,128)(2,1)S(1)} fusion(bf16[2,512,1536]{2,1,0:T(8,128)(2,1)} %get-tuple-element.212, bf16[3072,2,128]{0,2,1:T(8,128)(2,1)} %get-tuple-element.251, s32[]{:T(128)S(6)} %select_n.247, f32[512,2]{0,1:T(2,128)S(1)} %bitcast.105), kind=kOutput, calls=%fused_computation.11.clone.1 | convolution fusion | flops 402915328 | bytes 4198404 | tf_op jit(solution)/shard_map/while/body/eval_jaxpr/hgk,khd->ghd/dot_general | solution.py:119
  215.0 4.6 %fusion.63 = f32[1536,512,2]{0,1,2:T(8,128)} fusion(bf16[2048,2,192]{2,0,1:T(8,128)(2,1)} %get-tuple-element.256, s32[]{:T(128)S(6)} %select_n.248, s32[]{:T(128)S(6)} %add.230, bf16[3072,64]{0,1:T(8,128)(2,1)S(1)} %get-tuple-element.258, s32[]{:T(128)S(6)} %select_n.247), kind=kOutput, calls=%fused_computation.14.clone.1 | convolution fusion | flops 201326592 | bytes 6750220 | tf_op jit(solution)/shard_map/while/body/eval_jaxpr/ghd,kd->hgk/dot_general | solution.py:112
  220.6 8.2 %fusion.64 = (f32[2,512]{1,0:T(2,128)S(1)}, bf16[2,512,1536]{2,1,0:T(8,128)(2,1)}) fusion(pred[512,1536]{1,0:T(8,128)(4,1)S(1)} %and_and_fusion.2, f32[1536,512,2]{0,1,2:T(8,128)} %fusion.63, bf16[3072,2,128]{0,2,1:T(8,128)(2,1)} %get-tuple-element.257, s32[]{:T(128)S(6)} %select_n.247, bf16[2048,2,192]{2,0,1:T(8,128)(2,1)} %get-tuple-element.256, ...), kind=kOutput, calls=%fused_computation.56.clone.1 | convolution fusion | flops 413664768 | bytes 12062728 | tf_op jit(solution)/shard_map/while/body/eval_jaxpr/sub | solution.py:117
  228.8 3.3 %fusion.65 = bf16[1,512,2,128]{1,3,2,0:T(8,128)(2,1)S(1)} fusion(bf16[2,512,1536]{2,1,0:T(8,128)(2,1)} %get-tuple-element.212, bf16[3072,2,128]{0,2,1:T(8,128)(2,1)} %get-tuple-element.251, s32[]{:T(128)S(6)} %select_n.247, f32[512,2]{0,1:T(2,128)S(1)} %bitcast.105), kind=kOutput, calls=%fused_computation.11.clone.1 | convolution fusion | flops 402915328 | bytes 4198404 | tf_op jit(solution)/shard_map/while/body/eval_jaxpr/hgk,khd->ghd/dot_general | solution.py:119
  234.2 4.6 %fusion.63 = f32[1536,512,2]{0,1,2:T(8,128)} fusion(bf16[2048,2,192]{2,0,1:T(8,128)(2,1)} %get-tuple-element.256, s32[]{:T(128)S(6)} %select_n.248, s32[]{:T(128)S(6)} %add.230, bf16[3072,64]{0,1:T(8,128)(2,1)S(1)} %get-tuple-element.258, s32[]{:T(128)S(6)} %select_n.247), kind=kOutput, calls=%fused_computation.14.clone.1 | convolution fusion | flops 201326592 | bytes 6750220 | tf_op jit(solution)/shard_map/while/body/eval_jaxpr/ghd,kd->hgk/dot_general | solution.py:112
  239.9 8.1 %fusion.64 = (f32[2,512]{1,0:T(2,128)S(1)}, bf16[2,512,1536]{2,1,0:T(8,128)(2,1)}) fusion(pred[512,1536]{1,0:T(8,128)(4,1)S(1)} %and_and_fusion.2, f32[1536,512,2]{0,1,2:T(8,128)} %fusion.63, bf16[3072,2,128]{0,2,1:T(8,128)(2,1)} %get-tuple-element.257, s32[]{:T(128)S(6)} %select_n.247, bf16[2048,2,192]{2,0,1:T(8,128)(2,1)} %get-tuple-element.256, ...), kind=kOutput, calls=%fused_computation.56.clone.1 | convolution fusion | flops 413664768 | bytes 12062728 | tf_op jit(solution)/shard_map/while/body/eval_jaxpr/sub | solution.py:117
  248.0 3.3 %fusion.65 = bf16[1,512,2,128]{1,3,2,0:T(8,128)(2,1)S(1)} fusion(bf16[2,512,1536]{2,1,0:T(8,128)(2,1)} %get-tuple-element.212, bf16[3072,2,128]{0,2,1:T(8,128)(2,1)} %get-tuple-element.251, s32[]{:T(128)S(6)} %select_n.247, f32[512,2]{0,1:T(2,128)S(1)} %bitcast.105), kind=kOutput, calls=%fused_computation.11.clone.1 | convolution fusion | flops 402915328 | bytes 4198404 | tf_op jit(solution)/shard_map/while/body/eval_jaxpr/hgk,khd->ghd/dot_general | solution.py:119
  253.5 4.6 %fusion.63 = f32[1536,512,2]{0,1,2:T(8,128)} fusion(bf16[2048,2,192]{2,0,1:T(8,128)(2,1)} %get-tuple-element.256, s32[]{:T(128)S(6)} %select_n.248, s32[]{:T(128)S(6)} %add.230, bf16[3072,64]{0,1:T(8,128)(2,1)S(1)} %get-tuple-element.258, s32[]{:T(128)S(6)} %select_n.247), kind=kOutput, calls=%fused_computation.14.clone.1 | convolution fusion | flops 201326592 | bytes 6750220 | tf_op jit(solution)/shard_map/while/body/eval_jaxpr/ghd,kd->hgk/dot_general | solution.py:112
  259.1 8.2 %fusion.64 = (f32[2,512]{1,0:T(2,128)S(1)}, bf16[2,512,1536]{2,1,0:T(8,128)(2,1)}) fusion(pred[512,1536]{1,0:T(8,128)(4,1)S(1)} %and_and_fusion.2, f32[1536,512,2]{0,1,2:T(8,128)} %fusion.63, bf16[3072,2,128]{0,2,1:T(8,128)(2,1)} %get-tuple-element.257, s32[]{:T(128)S(6)} %select_n.247, bf16[2048,2,192]{2,0,1:T(8,128)(2,1)} %get-tuple-element.256, ...), kind=kOutput, calls=%fused_computation.56.clone.1 | convolution fusion | flops 413664768 | bytes 12062728 | tf_op jit(solution)/shard_map/while/body/eval_jaxpr/sub | solution.py:117
  267.3 3.3 %fusion.65 = bf16[1,512,2,128]{1,3,2,0:T(8,128)(2,1)S(1)} fusion(bf16[2,512,1536]{2,1,0:T(8,128)(2,1)} %get-tuple-element.212, bf16[3072,2,128]{0,2,1:T(8,128)(2,1)} %get-tuple-element.251, s32[]{:T(128)S(6)} %select_n.247, f32[512,2]{0,1:T(2,128)S(1)} %bitcast.105), kind=kOutput, calls=%fused_computation.11.clone.1 | convolution fusion | flops 402915328 | bytes 4198404 | tf_op jit(solution)/shard_map/while/body/eval_jaxpr/hgk,khd->ghd/dot_general | solution.py:119
  271.5 2.8 copy.48
  274.3 42.0 %all_to_all.37 = bf16[2048,2,128]{2,1,0:T(2,128)(2,1)S(1)} all-to-all(bf16[2048,2,128]{2,1,0:T(2,128)(2,1)S(1)} %copy.48), channel_id=1, replica_groups=mesh['blk'=16,'head_0'=8,'head_1'=2,'head_2'=2] {'head_0','head_1','head..., dimensions={0} | all-to-all | bytes 2097152 | tf_op jit(solution)/shard_map/all_to_all | solution.py:129
  (87 shorter events, 32.3 us)
Async XLA Ops:
  6.5 178.5 %copy-start = (bf16[512,256]{1,0:T(8,128)(2,1)S(1)}, bf16[512,256]{1,0:T(8,128)(2,1)}, u32[]{:S(2)}) copy-start(bf16[512,256]{1,0:T(8,128)(2,1)} %param.13) | copy-start | bytes 786436
  6.5 54.2 %all-gather.23.cloned.1.call-start = ((), (), s32[]{:S(2)}) async-start(), calls=%async_computation.5 | async-start | bytes 1474560 | tf_op jit(solution)/shard_map/all_gather | solution.py:35
  20.6 86.2 %all-gather.19.cloned.1.call-start = ((), (), s32[]{:S(2)}) async-start(), calls=%async_computation.3 | async-start | bytes 1474560 | tf_op jit(solution)/shard_map/all_gather | solution.py:35
  20.7 5.2 %collective-permute-start = (bf16[64,576]{1,0:T(8,128)(2,1)}, bf16[64,576]{1,0:T(8,128)(2,1)S(1)}, u32[]{:S(2)}, u32[]{:S(2)}) collective-permute-start(bf16[64,576]{1,0:T(8,128)(2,1)} %param.10), channel_id=1, source_target_pairs={{0,32},{32,64},{64,96},{96,128},{128,160},{160,192},{192,224},{224... | collective-permute-start | bytes 221192 | tf_op jit(solution)/shard_map/ppermute | solution.py:23
  33.8 146.5 %all-gather.25.cloned.1.call-start = ((), (), s32[]{:S(2)}) async-start(), calls=%async_computation.6 | async-start | bytes 3932160 | tf_op jit(solution)/shard_map/all_gather | solution.py:35
  62.3 26.5 %all-to-all-start.1 = ((s32[32,1,128]{2,1,0:T(1,128)}), s32[32,1,128]{2,1,0:T(1,128)S(1)}, u32[]{:S(2)}, u32[]{:S(2)}) async-start(s32[32,1,128]{2,1,0:T(1,128)} %reshape.246), calls=%async_computation.1 | async-start | bytes 32768 | tf_op jit(solution)/shard_map/all_to_all | solution.py:60
  83.2 23.6 %copy-start.2 = (s32[64]{0:T(128)S(1)}, s32[64]{0:T(128)}, u32[]{:S(2)}) copy-start(s32[64]{0:T(128)} %param.11) | copy-start | bytes 772
  88.8 88.3 %all-to-all-start = ((bf16[64,64,192]{2,0,1:T(8,128)(2,1)}), bf16[64,64,192]{2,0,1:T(8,128)(2,1)S(1)}, u32[]{:S(2)}, u32[]{:S(2)}) async-start(bf16[64,64,192]{2,0,1:T(8,128)(2,1)} %copy.41), calls=%async_computation | async-start | bytes 4194304 | tf_op jit(solution)/shard_map/all_to_all | solution.py:59
  95.5 86.8 %all-gather.21.cloned.1.call-start = ((), (), s32[]{:S(2)}) async-start(), calls=%async_computation.4 | async-start | bytes 3932160 | tf_op jit(solution)/shard_map/all_gather | solution.py:35
  106.9 5.3 %collective-permute-start.1 = (s32[64]{0:T(128)S(1)}, s32[64]{0:T(128)S(1)}, u32[]{:S(2)}, u32[]{:S(2)}) collective-permute-start(s32[64]{0:T(128)S(1)} %copy-done.2), channel_id=1, source_target_pairs={{0,32},{32,64},{64,96},{96,128},{128,160},{160,192},{192,224},{224... | collective-permute-start | bytes 776 | tf_op jit(solution)/shard_map/ppermute | solution.py:23
  185.0 4.0 %copy-start.1 = (bf16[512,256]{1,0:T(8,128)(2,1)S(1)}, bf16[512,256]{1,0:T(8,128)(2,1)}, u32[]{:S(2)}) copy-start(bf16[512,256]{1,0:T(8,128)(2,1)} %param.12) | copy-start | bytes 786436
Sparse Core Ops, SparseCore 0:
  20.8 39.9 all-gather.22
  62.8 43.9 all-gather.18
  108.9 29.6 all-gather.24
  140.6 20.7 all-gather.20
where the time goes:
time: 327 us; the launch traced here: 326 us
  blocking collectives  127 us (39%)
  matrix products  71.9 us (22%)
  waiting for transfers between devices  45.5 us (14%)
  local copies, waits for them, and re-layouts  28.6 us (9%)
  starting transfers between devices  28.1 us (9%)
  between operations  14 us (4%)
  other arithmetic  8.04 us (2%)
    all_gather x6, blocking collectives, all_blocks(): blocks = lax.all_gather(blocks, axes[k])  70.2 us
    all_to_all x1, blocking collectives, body(): lax.all_to_all(result, HEAD, split_axis=0, concat_axis=1, tiled=True)  42 us
    all_gather x4, waiting for transfers between devices, all_blocks(): blocks = lax.all_gather(blocks, axes[k])  38.1 us
    sub x4, matrix products, one_block(): weights = jnp.where(allowed[None], jnp.exp(scores - largest), 0.0)  32.6 us
    dot_general x4, matrix products, one_block(): jnp.einsum('ghd,kd->hgk', query_rope, rope_rows, preferred_element_type=j...  18.2 us
    all_to_all x1, starting transfers between devices, body(): lax.all_to_all(exponents, HEAD, split_axis=1, concat_axis=0, tiled=True)  14.8 us
    unnamed x1, blocking collectives  14.6 us
    dot_general x4, matrix products, one_block(): jnp.einsum('hgk,khd->ghd', weights.astype(jnp.bfloat16), value_rows, pref...  13.1 us
  transfers between devices with their start and end apart: 8, of which 4 were waited for; matrix products, arithmetic and copies ran while one was open for 5% of the time, Pallas kernels for 0%

commit v1 on v0

v1 whole, which is shorter than its diff:
```python
import math

import jax
import jax.numpy as jnp
from jax import lax
from jax.experimental import pallas as pl
from jax.experimental.pallas import tpu as pltpu
from jax.sharding import PartitionSpec as P

NOPE = 128
ROPE = 64
LATENT = 512
VDIM = 128
WIDE = 640
ROWS = 64
CHIP = 128
WINDOW = 1152
BIG = 1e30
BF = jnp.bfloat16
F32 = jnp.float32


def kernel(
    q_ref, e_ref, lat_ref, kw_ref, vw_ref, out_ref,
    wb, q2, ev, lat, kr, obuf, pw, noth, causal,
    local_sem, sib_send, sib_recv, z_send, z_recv, lat_send, lat_recv, latsib_send, latsib_recv,
    ring_send, ring_recv, out_send, out_recv,
):
    blk = lax.axis_index("blk")
    head = lax.axis_index("head")
    n_blk = lax.axis_size("blk")
    y, zh, c = head // 4, (head // 2) % 2, head % 2

    def at(b, yy, zz, cc):
        return {"blk": b, "head": yy * 4 + zz * 2 + cc}

    sibling = at(blk, y, zh, 1 - c)
    partner = at(blk, y, 1 - zh, c)
    up = at(blk, (y + 1) % 8, zh, c)
    down = at(blk, (y + 7) % 8, zh, c)
    later = at((blk + (y + 1) // 8) % n_blk, (y + 1) % 8, zh, c)
    earlier = at((blk + n_blk - (8 - y) // 8) % n_blk, (y + 7) % 8, zh, c)

    barrier = pltpu.get_barrier_semaphore()
    for other in (sibling, partner, up, down, later, earlier):
        pl.semaphore_signal(barrier, inc=1, device_id=other)
    pl.semaphore_wait(barrier, 6)

    def remote(src, dst, send, recv, device):
        return pltpu.make_async_remote_copy(
            src_ref=src, dst_ref=dst, send_sem=send, recv_sem=recv, device_id=device
        )

    own_lat = remote(lat_ref, lat.at[4, zh, c], z_send.at[0], z_recv.at[0], partner)
    own_lat.start()
    keep_lat = pltpu.make_async_copy(lat_ref, lat.at[4, zh, c], local_sem.at[0])
    keep_lat.start()
    wk_out = remote(kw_ref, wb.at[y, zh, pl.ds(0, 512)], z_send.at[1], z_recv.at[1], partner)
    wk_out.start()
    wv_out = remote(vw_ref, wb.at[y, zh, pl.ds(512, 512)], z_send.at[2], z_recv.at[2], partner)
    wv_out.start()
    wk_keep = pltpu.make_async_copy(kw_ref, wb.at[y, zh, pl.ds(0, 512)], local_sem.at[1])
    wk_keep.start()
    wv_keep = pltpu.make_async_copy(vw_ref, wb.at[y, zh, pl.ds(512, 512)], local_sem.at[2])
    wv_keep.start()
    my_rows = pl.ds(pl.multiple_of(c * ROWS, ROWS), ROWS)
    other_rows = pl.ds(pl.multiple_of((1 - c) * ROWS, ROWS), ROWS)
    e_keep = pltpu.make_async_copy(e_ref, ev.at[my_rows], local_sem.at[3])
    e_keep.start()
    e_out = remote(e_ref, ev.at[my_rows], sib_send.at[0], sib_recv.at[0], sibling)
    e_out.start()

    def q_columns(pair):
        return pl.ds(pl.multiple_of(pair * 384, 384), 384)

    def q_start(j, carry):
        pltpu.make_async_copy(
            q_ref.at[:, q_columns(2 * j + c)], q2.at[j, my_rows], local_sem.at[4]
        ).start()
        remote(
            q_ref.at[:, q_columns(2 * j + 1 - c)], q2.at[j, my_rows],
            sib_send.at[1], sib_recv.at[1], sibling,
        ).start()
        return carry

    lax.fori_loop(0, 16, q_start, 0)

    own_lat.wait()
    keep_lat.wait()
    steps = []
    for k in range(4):
        step = remote(
            lat.at[4 - k, :, c], lat.at[3 - k, :, c], lat_send.at[k], lat_recv.at[k], later
        )
        step.start()
        share = remote(
            lat.at[4 - k, :, c], lat.at[4 - k, :, c], latsib_send.at[k], latsib_recv.at[k], sibling
        )
        share.start()
        steps.append(step)
        steps.append(share)
        if k == 0:
            wk_out.wait()
            wv_out.wait()
            wk_keep.wait()
            wv_keep.wait()
            remote(wb.at[y], wb.at[y], ring_send.at[0], ring_recv.at[0], up).start()
            remote(wb.at[y], wb.at[y], ring_send.at[4], ring_recv.at[4], down).start()
        if k == 1:
            e_keep.wait()
            e_out.wait()
            powers = jnp.zeros((CHIP, 64), F32)
            for level in range(-4, 5):
                powers = powers + jnp.where(ev[...] == level, F32(2.0**level), F32(0.0))
            pw[...] = powers.astype(BF)
            causal[...] = jnp.where(
                lax.broadcasted_iota(jnp.int32, (CHIP, CHIP), 1)
                <= lax.broadcasted_iota(jnp.int32, (CHIP, CHIP), 0),
                F32(0.0), F32(-BIG),
            )
            pltpu.make_async_copy(
                q2.at[:, my_rows], q2.at[:, my_rows], local_sem.at[4]
            ).wait()
            remote(
                q2.at[:, my_rows], q2.at[:, other_rows], sib_send.at[1], sib_recv.at[1], sibling
            ).wait()
        step.wait_recv()
    last = remote(lat.at[0, :, c], lat.at[0, :, c], latsib_send.at[4], latsib_recv.at[4], sibling)
    last.start()
    for k in range(4):
        steps[2 * k + 1].wait_recv()
    last.wait_recv()

    def chip_rows(slot):
        block = lat[slot // 2, slot % 2]
        return block.reshape(CHIP, WIDE)

    tail = jnp.concatenate(
        [chip_rows(zh + k)[:, LATENT:] for k in range(9)], axis=0
    )
    kr[0, :, NOPE:] = tail
    kr[1, :, NOPE:] = tail
    lane = lax.broadcasted_iota(jnp.int32, (CHIP, CHIP), 1)
    own_tail = chip_rows(zh + 8)[:, LATENT:].astype(F32)
    noth[...] = jnp.where(lane < ROPE, F32(0.0), (own_tail - 1.0) * F32(BIG))
    scale = F32(math.log2(math.e) / math.sqrt(NOPE + ROPE))

    def one_pair(t, carry):
        n = t // 2
        odd = n % 2
        k = (n + 1) // 2
        yy = (y + 8 + jnp.where(odd == 1, -k, k)) % 8
        zz = t % 2
        j = yy * 2 + zz
        pair = 2 * j + c

        @pl.when((zz == 0) & (odd == 1))
        def _():
            remote(wb.at[yy], wb.at[yy], ring_send.at[k - 1], ring_recv.at[k - 1], up).wait_recv()

            @pl.when(k < 4)
            def _():
                remote(wb.at[yy], wb.at[yy], ring_send.at[k], ring_recv.at[k], up).start()

        @pl.when((zz == 0) & (odd == 0) & (k > 0))
        def _():
            remote(wb.at[yy], wb.at[yy], ring_send.at[k + 3], ring_recv.at[k + 3], down).wait_recv()

            @pl.when(k < 3)
            def _():
                remote(wb.at[yy], wb.at[yy], ring_send.at[k + 4], ring_recv.at[k + 4], down).start()

        latents = jnp.concatenate(
            [chip_rows(zh + k)[:, :LATENT] for k in range(9)], axis=0
        )
        keys = jnp.dot(latents, wb[yy, zz, :LATENT, :], preferred_element_type=F32).astype(BF)
        values = jnp.dot(latents, wb[yy, zz, LATENT:, :], preferred_element_type=F32).astype(BF)
        kr[0, :, :NOPE] = keys[:, :NOPE]
        kr[1, :, :NOPE] = keys[:, NOPE:]
        pick = jnp.where(
            lax.broadcasted_iota(jnp.int32, (64, 384), 0)
            == 2 * pair + (lax.broadcasted_iota(jnp.int32, (64, 384), 1) >= 192).astype(jnp.int32),
            F32(1.0), F32(0.0),
        ).astype(BF)
        scaled = q2[j].astype(F32) * jnp.dot(pw[...], pick, preferred_element_type=F32)
        turned = pltpu.roll(scaled, 320, 1)
        queries = [
            jnp.concatenate(
                [scaled[:, :128], jnp.where(lane < ROPE, scaled[:, 128:256], noth[...])], axis=1
            ).astype(BF),
            jnp.concatenate(
                [turned[:, 128:256], jnp.where(lane < ROPE, turned[:, 256:], noth[...])], axis=1
            ).astype(BF),
        ]
        for h in range(2):
            scores = lax.dot_general(
                queries[h], kr[h], (((1,), (1,)), ((), ())), preferred_element_type=F32
            )
            scores = jnp.concatenate(
                [scores[:, : WINDOW - CHIP], scores[:, WINDOW - CHIP :] + causal[...]], axis=1
            )
            largest = jnp.max(scores, axis=1, keepdims=True)
            weights = jnp.exp2((scores - largest) * scale)
            sums = jnp.sum(weights, axis=1, keepdims=True)
            weighted = jnp.dot(
                weights.astype(BF), values[:, h * VDIM : (h + 1) * VDIM],
                preferred_element_type=F32,
            )
            obuf[j, :, h * VDIM : (h + 1) * VDIM] = (weighted / sums).astype(BF)
        columns = pl.ds(pl.multiple_of(pair * 256, 256), 256)
        out_ref[:, columns] = obuf[j, my_rows, :]
        remote(
            obuf.at[j, other_rows], out_ref.at[:, columns], out_send.at[j], out_recv.at[j], sibling
        ).start()
        return carry

    lax.fori_loop(0, 16, one_pair, 0)

    def finish(j, carry):
        columns = pl.ds(pl.multiple_of((2 * j + 1 - c) * 256, 256), 256)
        remote(
            obuf.at[j, other_rows], out_ref.at[:, columns], out_send.at[j], out_recv.at[j], sibling
        ).wait()
        return carry

    lax.fori_loop(0, 16, finish, 0)
    for step in steps:
        step.wait_send()
    last.wait_send()
    for k in range(7):
        remote(wb.at[y], wb.at[y], ring_send.at[k], ring_recv.at[k], up).wait_send()


def body(queries, exponents, latent, segments, key_weight, value_weight):
    documents = (segments[:, None] == jnp.arange(64, dtype=jnp.int32)[None, :]).astype(BF)
    wide = jnp.concatenate([latent, documents], axis=1)
    hbm = pl.BlockSpec(memory_space=pl.ANY)
    dma = pltpu.SemaphoreType.DMA
    return pl.pallas_call(
        kernel,
        out_shape=jax.ShapeDtypeStruct((ROWS, 8192), BF),
        in_specs=[hbm] * 5,
        out_specs=pl.BlockSpec(memory_space=pltpu.VMEM),
        scratch_shapes=[
            pltpu.VMEM((8, 2, 1024, 256), BF),
            pltpu.VMEM((16, CHIP, 384), BF),
            pltpu.VMEM((CHIP, 64), jnp.int32),
            pltpu.VMEM((5, 2, 2, ROWS, WIDE), BF),
            pltpu.VMEM((2, WINDOW, 256), BF),
            pltpu.VMEM((16, CHIP, 256), BF),
            pltpu.VMEM((CHIP, 64), BF),
            pltpu.VMEM((CHIP, CHIP), F32),
            pltpu.VMEM((CHIP, CHIP), F32),
            dma((5,)),
            dma((2,)), dma((2,)),
            dma((3,)), dma((3,)),
            dma((4,)), dma((4,)),
            dma((5,)), dma((5,)),
            dma((7,)), dma((7,)),
            dma((16,)), dma((16,)),
        ],
        compiler_params=pltpu.CompilerParams(
            collective_id=0, has_side_effects=True, vmem_limit_bytes=52 * 1024 * 1024
        ),
    )(queries, exponents, wide, key_weight, value_weight)


def solution(mesh):
    both = ("blk", "head")
    placed = (
        P(both, None), P(both, None), P(both, None), P(both), P(None, "head"), P(None, "head"),
    )
    return jax.shard_map(
        body, mesh=mesh, in_specs=placed, out_specs=P(both, None), check_vma=False
    )
```

time: 327 us -> 171 us (0.52)
  the two profiles are of different devices: /device:TPU:1 before, /device:TPU:25 now
where the time goes in v1:
time: 171 us
  Pallas kernels  166 us (97%)
  local copies, waits for them, and re-layouts  3.63 us (2%)
    pallas_call x1, Pallas kernels, body(): pl.pallas_call(kernel, out_shape=jax.ShapeDtypeStruct((ROWS, 8192), BF),...  166 us
    unnamed x7, local copies, waits for them, and re-layouts  3.63 us

profile of v1, /device:TPU:25, one launch (start us, length us, event | category | flops | bytes accessed | tf_op | source)
XLA Modules:
  0.0 171.0 jit_solution(5544491314287840015)
XLA Ops:
  0.0 0.7 fusion
  0.7 1.0 pad_maximum_fusion.lat_ref
  1.7 0.0 copy-start
  1.7 0.9 copy-done
  2.7 0.0 copy-start.1
  2.7 0.9 copy-done.1
  3.6 0.0 copy-start.2
  3.6 0.8 copy-done.2
  4.4 165.6 %shard_map.64 = bf16[64,8192]{1,0:T(8,128)(2,1)S(1)} custom-call(bf16[64,12288]{1,0:T(8,128)(2,1)} %q_ref.1, s32[64,64]{1,0:T(8,128)S(1)} %copy-done.2, bf16[64,640]{1,0:T(8,128)(2,1)S(1)} %pad_maximum_fusion.lat_ref, bf16[512,256]{1,0:T(8,128)(2,1)S(1)} %copy-done, bf16[512,256]{1,0:T(8,128)(2,1)S(1)} %copy-done.1), custom_call_target="tpu_custom_call" | custom-call | tf_op jit(solution)/shard_map/pallas_call | solution.py:239
  170.0 1.0 copy.8
Async XLA Ops:
  1.7 0.9 copy-start
  2.7 0.9 copy-start.1
  3.6 0.8 copy-start.2

commit v2 on v1

v2 whole, which is shorter than its diff:
```python
import math

import jax
import jax.numpy as jnp
from jax import lax
from jax.experimental import pallas as pl
from jax.experimental.pallas import tpu as pltpu
from jax.sharding import PartitionSpec as P

NOPE = 128
ROPE = 64
LATENT = 512
VDIM = 128
WIDE = 640
ROWS = 64
CHIP = 128
WINDOW = 1152
UNION = 1408
BIG = 1e30
SPLIT = 2
BF = jnp.bfloat16
F32 = jnp.float32


def kernel(
    q_ref, e_ref, lat_ref, seg_ref, kw_ref, vw_ref, out_ref,
    wn, wf, wcur, q2, ev, lat, own, seg, kr, obuf, pw, noth, causal,
    local_sem, q_send, q_recv, e_send, e_recv, lat_send, lat_recv, share_send, share_recv,
    quarter_send, quarter_recv, spread_send, spread_recv,
    az_send, az_recv, ax_send, ax_recv, bz_send, bz_recv, bx_send, bx_recv, out_send, out_recv,
):
    blk = lax.axis_index("blk")
    head = lax.axis_index("head")
    n_blk = lax.axis_size("blk")
    zl, x = blk // 4, blk % 4
    y, zh, c = head // 4, (head // 2) % 2, head % 2
    z = zh * 4 + zl
    a = y % 2
    mate = (y + 1 - 2 * a) % 8

    def remote(src, dst, send, recv, device):
        return pltpu.make_async_remote_copy(
            src_ref=src, dst_ref=dst, send_sem=send, recv_sem=recv, device_id=device
        )

    def at(b, yy, zz, cc):
        return {"blk": b, "head": yy * 4 + zz * 2 + cc}

    def along_x(d):
        return at(zl * 4 + (x + d) % 4, y, zh, c)

    def along_y(d):
        return at(blk, (y + d) % 8, zh, c)

    def along_z(d):
        other = (z + d) % 8
        return at(other % 4 * 4 + x, y, other // 4, c)

    def onward(d):
        return at((blk + n_blk + (y + d + 8) // 8 - 1) % n_blk, (y + d + 8) % 8, zh, c)

    team = [(a, 1 - c), (1 - a, c), (1 - a, 1 - c)]
    team_at = [at(blk, y, zh, 1 - c), at(blk, mate, zh, c), at(blk, mate, zh, 1 - c)]
    extra_at = at(
        (blk + jnp.where(a == 0, (y + 5) // 8, 0)) % n_blk,
        jnp.where(a == 0, (y + 5) % 8, mate), zh, c,
    )
    extra_from = at(
        (blk + n_blk - jnp.where(a == 0, 0, (12 - y) // 8)) % n_blk,
        jnp.where(a == 0, mate, (y + 3) % 8), zh, c,
    )

    def token_rows(aa, cc):
        return pl.ds(pl.multiple_of((aa * 2 + cc) * ROWS, ROWS), ROWS)

    my_rows = token_rows(a, c)

    lat_in = pltpu.make_async_copy(lat_ref, own, local_sem.at[0])
    lat_in.start()
    seg_in = pltpu.make_async_copy(seg_ref, seg, local_sem.at[5])
    seg_in.start()
    wk_in = pltpu.make_async_copy(kw_ref, wn.at[zh, pl.ds(0, 512)], local_sem.at[1])
    wk_in.start()
    wv_in = pltpu.make_async_copy(vw_ref, wn.at[zh, pl.ds(512, 512)], local_sem.at[2])
    wv_in.start()
    e_in = pltpu.make_async_copy(e_ref, ev.at[my_rows], local_sem.at[3])
    e_in.start()

    def pair_of(j, aa, cc):
        return ((2 * (j // 2) + aa) * 2 + j % 2) * 2 + cc

    def q_columns(pair):
        return pl.ds(pl.multiple_of(pair * 384, 384), 384)

    def q_keep(j, carry):
        pltpu.make_async_copy(
            q_ref.at[:, q_columns(pair_of(j, a, c))], q2.at[j, my_rows], local_sem.at[4]
        ).start()
        return carry

    lax.fori_loop(0, 8, q_keep, 0)

    barrier = pltpu.get_barrier_semaphore()
    others = team_at + [extra_at, extra_from, onward(1), onward(-1), onward(4), onward(-4)]
    others += [along_x(d) for d in (1, 2, 3)]
    others += [along_y(d) for d in (2, 4, 6)] + [along_z(d) for d in (1, 4, 7)]
    for other in others:
        pl.semaphore_signal(barrier, inc=1, device_id=other)

    lat_in.wait()
    seg_in.wait()
    ids = lax.broadcasted_iota(jnp.int32, (CHIP, CHIP), 0)
    numbers = jnp.concatenate([seg[...], seg[...]], axis=1)
    hot = jnp.where(jnp.broadcast_to(numbers, (CHIP, CHIP)) == ids, F32(1.0), F32(0.0))
    hot = hot.T[:ROWS, :ROWS].astype(BF)
    lat[4 + a, zh, c] = jnp.concatenate([own[...], hot], axis=1)
    pl.semaphore_wait(barrier, len(others))

    def lat_pair():
        part = lat.at[4 + a, zh, c]
        return remote(part, part, lat_send.at[5], lat_recv.at[5], along_z(4))

    def lat_step(k):
        return remote(
            lat.at[4 + a - k, :, c], lat.at[4 - a - k, :, c], lat_send.at[k], lat_recv.at[k],
            onward(1),
        )

    def lat_four():
        return remote(
            lat.at[4 + a, :, c], lat.at[a, :, c], lat_send.at[3], lat_recv.at[3], onward(4)
        )

    def lat_extra():
        return remote(
            lat.at[4 + a, :, c], lat.at[5 * a, :, c], lat_send.at[4], lat_recv.at[4], extra_at
        )

    def share(k):
        slot = 5 - 5 * a if k == 5 else 4 + a - k
        part = lat.at[slot, :, c]
        return remote(part, part, share_send.at[k], share_recv.at[k], team_at[0])

    def q_part(r, zz, i):
        j = (y // 2 + r) % 4 * 2 + zz
        return remote(
            q_ref.at[:, q_columns(pair_of(j, team[i][0], team[i][1]))], q2.at[j, my_rows],
            q_send.at[r * 3 + i], q_recv.at[r * 3 + i], team_at[i],
        )

    def q_both(r, i):
        part = q2.at[pl.ds((y // 2 + r) % 4 * 2, 2), my_rows]
        return remote(part, part, q_send.at[r * 3 + i], q_recv.at[r * 3 + i], team_at[i])

    def q_start(r):
        for i in range(3):
            for zz in range(2):
                q_part(r, zz, i).start()

    def e_part(i):
        return remote(e_ref, ev.at[my_rows], e_send.at[i], e_recv.at[i], team_at[i])

    def quarter(mine):
        part = wn.at[zh if mine else 1 - zh, pl.ds(pl.multiple_of(x * 256, 256), 256)]
        return part

    def quarter_pair():
        return remote(
            quarter(True), quarter(True), quarter_send.at[3], quarter_recv.at[3], along_z(4)
        )

    def quarter_on(d):
        return remote(
            quarter(False), quarter(False), quarter_send.at[d - 1], quarter_recv.at[d - 1],
            along_x(d),
        )

    piece = pl.ds(pl.multiple_of((zl * 4 + x) * 64, 64), 64)

    def spread(d):
        return remote(
            wn.at[zh, piece], wf.at[z, x, 3 - d // 2], spread_send.at[0], spread_recv.at[0],
            along_y(d),
        )

    def spread_all():
        part = wf.at[z, x]
        return remote(part, part, spread_send.at[0], spread_recv.at[0], along_y(2))

    def az(way, k):
        held = (z + (9 - k if way == 0 else 7 + k)) % 8
        part = wf.at[held, x, pl.ds(0, SPLIT)]
        i = way * 4 + k - 1
        return remote(part, part, az_send.at[i], az_recv.at[i], along_z(1 if way == 0 else 7))

    def ax(offset, d):
        part = wf.at[(z + offset) % 8, x, pl.ds(0, SPLIT)]
        return remote(part, part, ax_send.at[d - 1], ax_recv.at[d - 1], along_x(d))

    def ax_all(d):
        part = wf.at[:, x, pl.ds(0, SPLIT)]
        return remote(part, part, ax_send.at[d - 1], ax_recv.at[d - 1], along_x(d))

    def bx(d):
        part = wf.at[z, x, pl.ds(SPLIT, 3 - SPLIT)]
        return remote(part, part, bx_send.at[d - 1], bx_recv.at[d - 1], along_x(d))

    def bz(way, k):
        held = (z + (9 - k if way == 0 else 7 + k)) % 8
        part = wf.at[held, :, pl.ds(SPLIT, 3 - SPLIT)]
        i = way * 4 + k - 1
        return remote(part, part, bz_send.at[i], bz_recv.at[i], along_z(1 if way == 0 else 7))

    def ax_start(offset):
        for d in (1, 3, 2):
            ax(offset, d).start()

    def a_begin():
        spread_all().wait_recv()
        az(0, 1).start()
        az(1, 1).start()
        for d in (1, 3, 2):
            bx(d).start()
        ax_start(0)

    def b_begin():
        for d in (1, 3, 2):
            bx(d).wait_recv()
        bz(0, 1).start()
        bz(1, 1).start()

    def a_next(k):
        az(1, k).wait_recv()
        if k < 4:
            az(1, k + 1).start()
            az(0, k).wait_recv()
            if k < 3:
                az(0, k + 1).start()
            ax_start(8 - k)
        ax_start(k)

    def b_next(k):
        bz(0, k).wait_recv()
        if k < 4:
            bz(0, k + 1).start()
            bz(1, k).wait_recv()
            if k < 3:
                bz(1, k + 1).start()

    def lat_next(k):
        lat_step(k).wait_recv()
        if k < 2:
            lat_step(k + 1).start()
        share(k + 1).start()

    lat_pair().start()
    wk_in.wait()
    wv_in.wait()
    for d in (4, 2, 6):
        spread(d).start()
    quarter_pair().start()
    for i in range(3):
        e_part(i).start()
    q_start(0)

    lat_pair().wait_recv()
    lat_step(0).start()
    lat_extra().start()
    lat_four().start()
    share(0).start()
    quarter_pair().wait_recv()
    for d in (1, 3, 2):
        quarter_on(d).start()
    a_begin()
    lat_next(0)
    b_begin()
    lat_next(1)
    a_next(1)
    q_start(1)
    lat_next(2)
    lat_four().wait_recv()
    share(4).start()
    lat_extra().wait_recv()
    share(5).start()
    q_start(2)
    q_start(3)
    a_next(2)
    b_next(1)
    e_in.wait()
    for i in range(3):
        e_part(i).wait_recv()
    powers = jnp.zeros((4 * ROWS, 64), F32)
    for level in range(-4, 5):
        powers = powers + jnp.where(ev[...] == level, F32(2.0**level), F32(0.0))
    pw[...] = powers.astype(BF)
    causal[...] = jnp.where(
        lax.broadcasted_iota(jnp.int32, (CHIP, CHIP), 1)
        <= lax.broadcasted_iota(jnp.int32, (CHIP, CHIP), 0),
        F32(0.0), F32(-BIG),
    )
    pltpu.make_async_copy(q2.at[:, my_rows], q2.at[:, my_rows], local_sem.at[4]).wait()
    for d in (1, 3, 2):
        quarter_on(d).wait_recv()
    for k in range(6):
        share(k).wait_recv()

    def chip_rows(slot):
        block = lat[slot // 2, slot % 2]
        return block.reshape(CHIP, WIDE)

    tail = jnp.concatenate([chip_rows(zh + k)[:, LATENT:] for k in range(11)], axis=0)
    kr[0, :, NOPE:] = tail
    kr[1, :, NOPE:] = tail
    lane = lax.broadcasted_iota(jnp.int32, (2 * CHIP, CHIP), 1)
    own_tail = jnp.concatenate([chip_rows(zh + k)[:, LATENT:] for k in (8, 10)], axis=0)
    noth[...] = jnp.where(lane < ROPE, F32(0.0), (own_tail.astype(F32) - 1.0) * F32(BIG))
    scale = F32(math.log2(math.e) / math.sqrt(NOPE + ROPE))

    def q_ready(r):
        for i in range(3):
            q_both(r, i).wait_recv()

    def far_a():
        for d in (1, 3, 2):
            ax_all(d).wait_recv()

    events = {
        0: [lambda: q_ready(0), lambda: a_next(3), lambda: b_next(2)],
        1: [lambda: a_next(4), lambda: b_next(3)],
        2: [lambda: q_ready(1), far_a],
        3: [lambda: b_next(4)],
        4: [lambda: q_ready(2)],
        6: [lambda: q_ready(3)],
    }

    def nt(left, right):
        return lax.dot_general(
            left, right, (((1,), (1,)), ((), ())), preferred_element_type=F32
        )

    def one_pair(t, carry):
        for when, todo in events.items():
            for event in todo:
                pl.when(t == when)(event)

        r = t // 2
        zz = (zh + t) % 2
        j = (y // 2 + r) % 4 * 2 + zz
        pair = pair_of(j, a, c)

        @pl.when(r > 0)
        def _():
            wcur[...] = wf[pl.ds(zz * 4, 4), :, jnp.maximum(r - 1, 0)].reshape(1024, 256)

        @pl.when(r == 0)
        def _():
            wcur[...] = wn[zz]

        latents = jnp.concatenate([chip_rows(zh + k)[:, :LATENT] for k in range(11)], axis=0)
        keys = jnp.dot(latents, wcur[:LATENT, :], preferred_element_type=F32).astype(BF)
        values = jnp.dot(latents, wcur[LATENT:, :], preferred_element_type=F32).astype(BF)
        kr[0, :, :NOPE] = keys[:, :NOPE]
        kr[1, :, :NOPE] = keys[:, NOPE:]
        pick = jnp.where(
            lax.broadcasted_iota(jnp.int32, (64, 384), 0)
            == 2 * pair + (lax.broadcasted_iota(jnp.int32, (64, 384), 1) >= 192).astype(jnp.int32),
            F32(1.0), F32(0.0),
        ).astype(BF)
        scaled = q2[j].astype(F32) * jnp.dot(pw[...], pick, preferred_element_type=F32)
        turned = pltpu.roll(scaled, 320, 1)
        queries = [
            jnp.concatenate(
                [scaled[:, :128], jnp.where(lane < ROPE, scaled[:, 128:256], noth[...])], axis=1
            ).astype(BF),
            jnp.concatenate(
                [turned[:, 128:256], jnp.where(lane < ROPE, turned[:, 256:], noth[...])], axis=1
            ).astype(BF),
        ]
        for h in range(2):
            both = nt(queries[h], kr[h, 256:WINDOW])
            first = nt(queries[h][:CHIP], kr[h, :256])
            last = nt(queries[h][CHIP:], kr[h, WINDOW:])
            scores = jnp.concatenate(
                [
                    jnp.concatenate([first, both[:CHIP]], axis=1),
                    jnp.concatenate([both[CHIP:], last], axis=1),
                ],
                axis=0,
            )
            mask = jnp.concatenate([causal[...], causal[...]], axis=0)
            scores = jnp.concatenate(
                [scores[:, : WINDOW - CHIP], scores[:, WINDOW - CHIP :] + mask], axis=1
            )
            largest = jnp.max(scores, axis=1, keepdims=True)
            weights = jnp.exp2((scores - largest) * scale)
            sums = jnp.sum(weights, axis=1, keepdims=True)
            weights = weights.astype(BF)
            for b in range(2):
                rows = slice(b * CHIP, (b + 1) * CHIP)
                weighted = jnp.dot(
                    weights[rows],
                    values[b * 256 : b * 256 + WINDOW, h * VDIM : (h + 1) * VDIM],
                    preferred_element_type=F32,
                )
                obuf[j, rows, h * VDIM : (h + 1) * VDIM] = (weighted / sums[rows]).astype(BF)
        columns = pl.ds(pl.multiple_of(pair * 256, 256), 256)
        for i in range(3):
            out_part(j, i, columns).start()
        out_ref[:, columns] = obuf[j, my_rows, :]
        return carry

    def out_part(j, i, columns):
        return remote(
            obuf.at[j, token_rows(team[i][0], team[i][1])], out_ref.at[:, columns],
            out_send.at[i * 8 + j], out_recv.at[i * 8 + j], team_at[i],
        )

    lax.fori_loop(0, 8, one_pair, 0)

    def finish(j, carry):
        for i in range(3):
            pair = pair_of(j, team[i][0], team[i][1])
            out_part(j, i, pl.ds(pl.multiple_of(pair * 256, 256), 256)).wait()
        return carry

    lax.fori_loop(0, 8, finish, 0)
    for i in range(3):
        e_part(i).wait_send()
        for r in range(4):
            q_both(r, i).wait_send()
    lat_pair().wait_send()
    lat_four().wait_send()
    lat_extra().wait_send()
    for k in range(3):
        lat_step(k).wait_send()
    for k in range(6):
        share(k).wait_send()
    quarter_pair().wait_send()
    spread_all().wait_send()
    for d in (1, 2, 3):
        quarter_on(d).wait_send()
        ax_all(d).wait_send()
        bx(d).wait_send()
    for k in range(1, 5):
        az(1, k).wait_send()
        bz(0, k).wait_send()
        if k < 4:
            az(0, k).wait_send()
            bz(1, k).wait_send()


def body(queries, exponents, latent, segments, key_weight, value_weight):
    documents = segments.reshape(1, ROWS)
    hbm = pl.BlockSpec(memory_space=pl.ANY)
    dma = pltpu.SemaphoreType.DMA
    return pl.pallas_call(
        kernel,
        out_shape=jax.ShapeDtypeStruct((ROWS, 8192), BF),
        in_specs=[hbm] * 6,
        out_specs=pl.BlockSpec(memory_space=pltpu.VMEM),
        scratch_shapes=[
            pltpu.VMEM((2, 1024, 256), BF),
            pltpu.VMEM((8, 4, 3, 64, 256), BF),
            pltpu.VMEM((1024, 256), BF),
            pltpu.VMEM((8, 4 * ROWS, 384), BF),
            pltpu.VMEM((4 * ROWS, 64), jnp.int32),
            pltpu.VMEM((6, 2, 2, ROWS, WIDE), BF),
            pltpu.VMEM((ROWS, 576), BF),
            pltpu.VMEM((1, ROWS), jnp.int32),
            pltpu.VMEM((2, UNION, 256), BF),
            pltpu.VMEM((8, 4 * ROWS, 256), BF),
            pltpu.VMEM((4 * ROWS, 64), BF),
            pltpu.VMEM((2 * CHIP, CHIP), F32),
            pltpu.VMEM((CHIP, CHIP), F32),
            dma((6,)),
            dma((12,)), dma((12,)),
            dma((3,)), dma((3,)),
            dma((6,)), dma((6,)),
            dma((6,)), dma((6,)),
            dma((4,)), dma((4,)),
            dma((1,)), dma((1,)),
            dma((8,)), dma((8,)),
            dma((3,)), dma((3,)),
            dma((8,)), dma((8,)),
            dma((3,)), dma((3,)),
            dma((24,)), dma((24,)),
        ],
        compiler_params=pltpu.CompilerParams(
            collective_id=0, has_side_effects=True, vmem_limit_bytes=58 * 1024 * 1024
        ),
    )(queries, exponents, latent, documents, key_weight, value_weight)


def solution(mesh):
    both = ("blk", "head")
    placed = (
        P(both, None), P(both, None), P(both, None), P(both), P(None, "head"), P(None, "head"),
    )
    return jax.shard_map(
        body, mesh=mesh, in_specs=placed, out_specs=P(both, None), check_vma=False
    )
```

time: 171 us -> 91.8 us (0.54)
  the two profiles are of different devices: /device:TPU:25 before, /device:TPU:1 now
where the time goes in v2:
time: 91.8 us; the launch traced here: 91.2 us
  Pallas kernels  88.9 us (97%)
  local copies, waits for them, and re-layouts  2.26 us (2%)
    pallas_call x1, Pallas kernels, body(): pl.pallas_call(kernel, out_shape=jax.ShapeDtypeStruct((ROWS, 8192), BF),...  88.9 us
    unnamed x1, local copies, waits for them, and re-layouts  2.26 us

profile of v2, /device:TPU:1, one launch (start us, length us, event | category | flops | bytes accessed | tf_op | source)
XLA Modules:
  0.0 91.2 jit_solution(4542314169170281555)
XLA Ops:
  0.0 88.9 %shard_map.64 = bf16[64,8192]{1,0:T(8,128)(2,1)} custom-call(bf16[64,12288]{1,0:T(8,128)(2,1)} %q_ref.1, s32[64,64]{1,0:T(8,128)} %e_ref.1, bf16[64,576]{1,0:T(8,128)(2,1)} %lat_ref.1, s32[1,64]{1,0:T(1,128)} %bitcast.1, bf16[512,256]{1,0:T(8,128)(2,1)} %kw_ref.1, bf16[512,256]{1,0:T(8,128)(2,1)} %vw_ref.1), custom_call_target="tpu_custom_call" | custom-call | tf_op jit(solution)/shard_map/pallas_call | solution.py:456
  88.9 2.3 %copy.8 = bf16[64,8192]{1,0:T(8,128)(2,1)} copy(bf16[64,8192]{1,0:T(8,128)(2,1)} %shard_map.64) | data formatting | bytes 2097152

commit v3 on v2

--- a/solution.py
+++ b/solution.py
@@ -17,7 +17,7 @@
 WINDOW = 1152
 UNION = 1408
 BIG = 1e30
-SPLIT = 2
+SPLIT = 112
 BF = jnp.bfloat16
 F32 = jnp.float32
 
@@ -101,7 +101,7 @@
     lax.fori_loop(0, 8, q_keep, 0)
 
     barrier = pltpu.get_barrier_semaphore()
-    others = team_at + [extra_at, extra_from, onward(1), onward(-1), onward(4), onward(-4)]
+    others = team_at + [extra_at, extra_from, onward(1), onward(-1)]
     others += [along_x(d) for d in (1, 2, 3)]
     others += [along_y(d) for d in (2, 4, 6)] + [along_z(d) for d in (1, 4, 7)]
     for other in others:
@@ -126,9 +126,9 @@
             onward(1),
         )
 
-    def lat_four():
-        return remote(
-            lat.at[4 + a, :, c], lat.at[a, :, c], lat_send.at[3], lat_recv.at[3], onward(4)
+    def lat_second():
+        return remote(
+            lat.at[5 - 5 * a, :, c], lat.at[1 - a, :, c], lat_send.at[3], lat_recv.at[3], extra_at
         )
 
     def lat_extra():
@@ -179,7 +179,7 @@
 
     def spread(d):
         return remote(
-            wn.at[zh, piece], wf.at[z, x, 3 - d // 2], spread_send.at[0], spread_recv.at[0],
+            wn.at[zh, piece], wf.at[z, x, pl.ds((3 - d // 2) * 64, 64)], spread_send.at[0], spread_recv.at[0],
             along_y(d),
         )
 
@@ -202,12 +202,12 @@
         return remote(part, part, ax_send.at[d - 1], ax_recv.at[d - 1], along_x(d))
 
     def bx(d):
-        part = wf.at[z, x, pl.ds(SPLIT, 3 - SPLIT)]
+        part = wf.at[z, x, pl.ds(SPLIT, 192 - SPLIT)]
         return remote(part, part, bx_send.at[d - 1], bx_recv.at[d - 1], along_x(d))
 
     def bz(way, k):
         held = (z + (9 - k if way == 0 else 7 + k)) % 8
-        part = wf.at[held, :, pl.ds(SPLIT, 3 - SPLIT)]
+        part = wf.at[held, :, pl.ds(SPLIT, 192 - SPLIT)]
         i = way * 4 + k - 1
         return remote(part, part, bz_send.at[i], bz_recv.at[i], along_z(1 if way == 0 else 7))
 
@@ -258,34 +258,33 @@
     wv_in.wait()
     for d in (4, 2, 6):
         spread(d).start()
-    quarter_pair().start()
-    for i in range(3):
-        e_part(i).start()
-    q_start(0)
-
     lat_pair().wait_recv()
     lat_step(0).start()
     lat_extra().start()
-    lat_four().start()
     share(0).start()
-    quarter_pair().wait_recv()
-    for d in (1, 3, 2):
-        quarter_on(d).start()
     a_begin()
+    for i in range(3):
+        e_part(i).start()
     lat_next(0)
+    a_next(1)
     b_begin()
+    lat_extra().wait_recv()
+    lat_second().start()
+    share(5).start()
+    a_next(2)
     lat_next(1)
-    a_next(1)
+    q_start(0)
+    b_next(1)
+    a_next(3)
+    lat_next(2)
+    a_next(4)
+    lat_second().wait_recv()
+    share(4).start()
     q_start(1)
-    lat_next(2)
-    lat_four().wait_recv()
-    share(4).start()
-    lat_extra().wait_recv()
-    share(5).start()
+    b_next(2)
+    quarter_pair().start()
     q_start(2)
     q_start(3)
-    a_next(2)
-    b_next(1)
     e_in.wait()
     for i in range(3):
         e_part(i).wait_recv()
@@ -299,8 +298,6 @@
         F32(0.0), F32(-BIG),
     )
     pltpu.make_async_copy(q2.at[:, my_rows], q2.at[:, my_rows], local_sem.at[4]).wait()
-    for d in (1, 3, 2):
-        quarter_on(d).wait_recv()
     for k in range(6):
         share(k).wait_recv()
 
@@ -324,13 +321,21 @@
         for d in (1, 3, 2):
             ax_all(d).wait_recv()
 
+    def quarter_next():
+        quarter_pair().wait_recv()
+        for d in (1, 3, 2):
+            quarter_on(d).start()
+
+    def quarter_done():
+        for d in (1, 3, 2):
+            quarter_on(d).wait_recv()
+
     events = {
-        0: [lambda: q_ready(0), lambda: a_next(3), lambda: b_next(2)],
-        1: [lambda: a_next(4), lambda: b_next(3)],
-        2: [lambda: q_ready(1), far_a],
-        3: [lambda: b_next(4)],
-        4: [lambda: q_ready(2)],
-        6: [lambda: q_ready(3)],
+        0: [lambda: q_ready(0), lambda: b_next(3)],
+        1: [quarter_next, lambda: q_ready(1), far_a],
+        3: [lambda: q_ready(2), lambda: b_next(4)],
+        5: [lambda: q_ready(3)],
+        7: [quarter_done],
     }
 
     def nt(left, right):
@@ -343,14 +348,15 @@
             for event in todo:
                 pl.when(t == when)(event)
 
-        r = t // 2
+        r = (t + 1) // 2 % 4
         zz = (zh + t) % 2
         j = (y // 2 + r) % 4 * 2 + zz
         pair = pair_of(j, a, c)
 
         @pl.when(r > 0)
         def _():
-            wcur[...] = wf[pl.ds(zz * 4, 4), :, jnp.maximum(r - 1, 0)].reshape(1024, 256)
+            start = pl.multiple_of(jnp.maximum(r - 1, 0) * 64, 64)
+            wcur[...] = wf[pl.ds(zz * 4, 4), :, pl.ds(start, 64)].reshape(1024, 256)
 
         @pl.when(r == 0)
         def _():
@@ -429,7 +435,7 @@
         for r in range(4):
             q_both(r, i).wait_send()
     lat_pair().wait_send()
-    lat_four().wait_send()
+    lat_second().wait_send()
     lat_extra().wait_send()
     for k in range(3):
         lat_step(k).wait_send()
@@ -460,7 +466,7 @@
         out_specs=pl.BlockSpec(memory_space=pltpu.VMEM),
         scratch_shapes=[
             pltpu.VMEM((2, 1024, 256), BF),
-            pltpu.VMEM((8, 4, 3, 64, 256), BF),
+            pltpu.VMEM((8, 4, 192, 256), BF),
             pltpu.VMEM((1024, 256), BF),
             pltpu.VMEM((8, 4 * ROWS, 384), BF),
             pltpu.VMEM((4 * ROWS, 64), jnp.int32),

time: 91.8 us -> 82.9 us (0.903)
  Pallas kernels: 88.9 us -> 80.4 us
    pallas_call x1, Pallas kernels: 88.9 us -> 80.4 us  [body(): pl.pallas_call(kernel, out_shape=jax.ShapeDtypeStruct((ROWS, 8192), BF),...]
where the time goes in v3:
time: 82.9 us; the launch traced here: 82.7 us
  Pallas kernels  80.4 us (97%)
  local copies, waits for them, and re-layouts  2.26 us (3%)
    pallas_call x1, Pallas kernels, body(): pl.pallas_call(kernel, out_shape=jax.ShapeDtypeStruct((ROWS, 8192), BF),...  80.4 us
    unnamed x1, local copies, waits for them, and re-layouts  2.26 us

profile of v3, /device:TPU:1, one launch (start us, length us, event | category | flops | bytes accessed | tf_op | source)
XLA Modules:
  0.0 82.7 jit_solution(1244689570426978946)
XLA Ops:
  0.0 80.4 %shard_map.64 = bf16[64,8192]{1,0:T(8,128)(2,1)} custom-call(bf16[64,12288]{1,0:T(8,128)(2,1)} %q_ref.1, s32[64,64]{1,0:T(8,128)} %e_ref.1, bf16[64,576]{1,0:T(8,128)(2,1)} %lat_ref.1, s32[1,64]{1,0:T(1,128)} %bitcast.1, bf16[512,256]{1,0:T(8,128)(2,1)} %kw_ref.1, bf16[512,256]{1,0:T(8,128)(2,1)} %vw_ref.1), custom_call_target="tpu_custom_call" | custom-call | tf_op jit(solution)/shard_map/pallas_call | solution.py:462
  80.4 2.3 %copy.8 = bf16[64,8192]{1,0:T(8,128)(2,1)} copy(bf16[64,8192]{1,0:T(8,128)(2,1)} %shard_map.64) | data formatting | bytes 2097152

commit v4 on v3

--- a/solution.py
+++ b/solution.py
@@ -17,7 +17,7 @@
 WINDOW = 1152
 UNION = 1408
 BIG = 1e30
-SPLIT = 112
+SPLIT = 128
 BF = jnp.bfloat16
 F32 = jnp.float32
 
@@ -258,31 +258,32 @@
     wv_in.wait()
     for d in (4, 2, 6):
         spread(d).start()
+    a_begin()
     lat_pair().wait_recv()
     lat_step(0).start()
     lat_extra().start()
     share(0).start()
-    a_begin()
+    a_next(1)
+    b_begin()
+    lat_next(0)
     for i in range(3):
         e_part(i).start()
-    lat_next(0)
-    a_next(1)
-    b_begin()
+    a_next(2)
+    b_next(1)
+    lat_next(1)
+    a_next(3)
     lat_extra().wait_recv()
     lat_second().start()
     share(5).start()
-    a_next(2)
-    lat_next(1)
     q_start(0)
-    b_next(1)
-    a_next(3)
+    a_next(4)
+    b_next(2)
     lat_next(2)
-    a_next(4)
     lat_second().wait_recv()
     share(4).start()
     q_start(1)
-    b_next(2)
     quarter_pair().start()
+    b_next(3)
     q_start(2)
     q_start(3)
     e_in.wait()
@@ -331,10 +332,10 @@
             quarter_on(d).wait_recv()
 
     events = {
-        0: [lambda: q_ready(0), lambda: b_next(3)],
+        0: [lambda: q_ready(0)],
         1: [quarter_next, lambda: q_ready(1), far_a],
-        3: [lambda: q_ready(2), lambda: b_next(4)],
-        5: [lambda: q_ready(3)],
+        3: [lambda: q_ready(2)],
+        5: [lambda: q_ready(3), lambda: b_next(4)],
         7: [quarter_done],
     }
 

time: 82.9 us -> 81.9 us (0.988)
  Pallas kernels: 80.4 us -> 78.9 us
    pallas_call x1, Pallas kernels: 80.4 us -> 78.9 us  [body(): pl.pallas_call(kernel, out_shape=jax.ShapeDtypeStruct((ROWS, 8192), BF),...]
where the time goes in v4:
time: 81.9 us; the launch traced here: 81.2 us
  Pallas kernels  78.9 us (96%)
  local copies, waits for them, and re-layouts  2.26 us (3%)
    pallas_call x1, Pallas kernels, body(): pl.pallas_call(kernel, out_shape=jax.ShapeDtypeStruct((ROWS, 8192), BF),...  78.9 us
    unnamed x1, local copies, waits for them, and re-layouts  2.26 us

profile of v4, /device:TPU:1, one launch (start us, length us, event | category | flops | bytes accessed | tf_op | source)
XLA Modules:
  0.0 81.2 jit_solution(557342913216724207)
XLA Ops:
  0.0 78.9 %shard_map.64 = bf16[64,8192]{1,0:T(8,128)(2,1)} custom-call(bf16[64,12288]{1,0:T(8,128)(2,1)} %q_ref.1, s32[64,64]{1,0:T(8,128)} %e_ref.1, bf16[64,576]{1,0:T(8,128)(2,1)} %lat_ref.1, s32[1,64]{1,0:T(1,128)} %bitcast.1, bf16[512,256]{1,0:T(8,128)(2,1)} %kw_ref.1, bf16[512,256]{1,0:T(8,128)(2,1)} %vw_ref.1), custom_call_target="tpu_custom_call" | custom-call | tf_op jit(solution)/shard_map/pallas_call | solution.py:463
  79.0 2.3 %copy.8 = bf16[64,8192]{1,0:T(8,128)(2,1)} copy(bf16[64,8192]{1,0:T(8,128)(2,1)} %shard_map.64) | data formatting | bytes 2097152
